TPU v7x, 256 devices: a whole 4x4x8 slice. The times are simulated.
256 devices in a mesh: dp: 16 (over y, x), expert: 16 (over z, core).
Axes of the slice: x: 4, y: 4, z: 8, core: 2. Of those that a mesh axis runs over, the one named last changes fastest.
Arguments:
- tokens: bfloat16 [8192, 2048], P('dp'), may hold values from -6 to 6
- routes: int32 [8192, 6], P('dp'), may hold values from 0 to 63, all different within a row; in each aligned block of 512 rows (0 to 511, 512 to 1023, ...) at most 72 rows name the same one
- route_weight: float32 [8192, 6], P('dp'), may hold values from 0.05 to 0.5
- w_gate: bfloat16 [256, 352, 2048], P(('dp', 'expert')), may hold values from -0.125 to 0.125
- w_up: bfloat16 [256, 352, 2048], P(('dp', 'expert')), may hold values from -0.125 to 0.125
- w_down: bfloat16 [256, 352, 2048], P(('dp', 'expert')), may hold values from -0.15625 to 0.15625
- grad_out: bfloat16 [8192, 2048], P(('dp', 'expert')), may hold values from -6 to 6
Outputs:
- mixed: bfloat16 [8192, 2048], P(('dp', 'expert'))
- grad_tokens: bfloat16 [8192, 2048], P(('dp', 'expert'))
- grad_route_weight: float32 [8192, 6], P(('dp', 'expert'))
- grad_gate: bfloat16 [256, 352, 2048], P(('dp', 'expert'))
- grad_up: bfloat16 [256, 352, 2048], P(('dp', 'expert'))
- grad_down: bfloat16 [256, 352, 2048], P(('dp', 'expert'))
Inputs may be any that keep to these rules, and one draw needn't show every extreme that they name: `routes`: each row names 6 different experts. Within the 512 rows of one index of dp no expert is named by more than 72 rows.
All inputs are finite; a program needn't handle non-finite values.
Results may differ from a plain program's by a relative error of at most 0.023.
Values may be sent and summed in bfloat16 or wider, within the bound.
A program may use at most 192 MiB of HBM per device.

v0:
```python
import jax
import jax.numpy as jnp
from jax import lax
from jax.sharding import PartitionSpec as P

SHARDS = 4


def silu_parts(gate_pre):
    sigma = jax.nn.sigmoid(gate_pre)
    return (gate_pre * sigma, sigma * (1.0 + gate_pre * (1.0 - sigma)))


def deliver(buffer):
    dp_count, slot_count, width = buffer.shape
    arrived = lax.all_to_all(buffer, "dp", split_axis=0, concat_axis=0, tiled=True)
    return arrived.reshape(dp_count * slot_count, width)


def send_back(rows, dp_count, slot_count):
    width = rows.shape[1]
    returned = lax.all_to_all(
        rows.reshape(dp_count, slot_count, width), "dp", split_axis=0, concat_axis=0, tiled=True
    )
    return (returned.reshape(dp_count * slot_count, width), jnp.zeros((), jnp.int32))


def body(tokens, routes, route_weight, w_gate, w_up, w_down, grad_out):
    dp_count = lax.axis_size("dp")
    ex_count = lax.axis_size("expert")
    groups = ex_count // SHARDS
    my_group = lax.axis_index("expert") // SHARDS
    tok_rows, top_count = routes.shape
    width = tokens.shape[1]
    expert_count = dp_count * groups
    capacity = min(tok_rows, 3 * tok_rows * top_count // (2 * expert_count))
    flat_routes = routes.reshape(-1)
    route_count = flat_routes.shape[0]
    owner_ids = jnp.arange(dp_count, dtype=jnp.int32) * groups + my_group
    hit_table = (flat_routes[:, None] == owner_ids[None, :]).astype(jnp.int32)
    is_live = jnp.sum(hit_table, axis=1)
    owner_dp = jnp.sum(hit_table * jnp.arange(dp_count, dtype=jnp.int32)[None, :], axis=1)
    slot_index = jnp.sum((jnp.cumsum(hit_table, axis=0) - 1) * hit_table, axis=1)
    dump_row = dp_count * capacity
    target = jnp.where(is_live == 1, owner_dp * capacity + slot_index, dump_row)
    source = (
        jnp.full((dump_row + 1,), route_count, jnp.int32)
        .at[target]
        .set(jnp.arange(route_count, dtype=jnp.int32))[:dump_row]
    )
    filled = source < route_count
    safe_source = jnp.where(filled, source, 0)
    token_of = safe_source // top_count
    weights_flat = route_weight.reshape(-1)
    send_rows = jnp.where(filled[:, None], tokens[token_of], jnp.zeros((), tokens.dtype))
    x_rows = deliver(send_rows.reshape(dp_count, capacity, width))
    gate_matrix = w_gate[0]
    up_matrix = w_up[0]
    down_matrix = w_down[0]
    gate_pre = jnp.einsum("rd,fd->rf", x_rows, gate_matrix, preferred_element_type=jnp.float32)
    up_pre = jnp.einsum("rd,fd->rf", x_rows, up_matrix, preferred_element_type=jnp.float32)
    silu_value, silu_slope = silu_parts(gate_pre)
    hidden = (silu_value * up_pre).astype(jnp.bfloat16)
    shard_part = jnp.dot(hidden, down_matrix, preferred_element_type=jnp.float32).astype(
        jnp.bfloat16
    )
    returned, offset = send_back(shard_part, dp_count, capacity)
    piece_width = returned.shape[1]
    safe_target = jnp.where(is_live == 1, target, 0)
    route_part = jnp.where(
        is_live[:, None] == 1, returned[safe_target], jnp.zeros((), returned.dtype)
    )
    weighted = weights_flat[:, None] * route_part.astype(jnp.float32)
    mixed_part = jnp.sum(weighted.reshape(tok_rows, top_count, piece_width), axis=1)
    cotangent = lax.all_gather(grad_out, "expert", axis=0, tiled=True)
    route_grad = jnp.sum(
        route_part.reshape(tok_rows, top_count, piece_width).astype(jnp.float32)
        * cotangent[:, None, :].astype(jnp.float32),
        axis=2,
    )
    weight_of = jnp.where(filled, weights_flat[safe_source], jnp.zeros((), weights_flat.dtype))
    send_cot = (weight_of[:, None] * cotangent[token_of].astype(jnp.float32)).astype(jnp.bfloat16)
    cot_rows = deliver(send_cot.reshape(dp_count, capacity, width))
    d_hidden = jnp.einsum("rd,fd->rf", cot_rows, down_matrix, preferred_element_type=jnp.float32)
    d_gate = (d_hidden * up_pre * silu_slope).astype(jnp.bfloat16)
    d_up = (d_hidden * silu_value).astype(jnp.bfloat16)
    grad_down = jnp.einsum(
        "rf,rd->fd", hidden, cot_rows, preferred_element_type=jnp.float32
    ).astype(jnp.bfloat16)[None]
    grad_gate = jnp.einsum("rf,rd->fd", d_gate, x_rows, preferred_element_type=jnp.float32).astype(
        jnp.bfloat16
    )[None]
    grad_up = jnp.einsum("rf,rd->fd", d_up, x_rows, preferred_element_type=jnp.float32).astype(
        jnp.bfloat16
    )[None]
    shard_dx = jnp.dot(d_gate, gate_matrix, preferred_element_type=jnp.float32) + jnp.dot(
        d_up, up_matrix, preferred_element_type=jnp.float32
    )
    dx_back, dx_offset = send_back(shard_dx.astype(jnp.bfloat16), dp_count, capacity)
    route_dx = jnp.where(is_live[:, None] == 1, dx_back[safe_target], jnp.zeros((), dx_back.dtype))
    dx_part = jnp.sum(
        route_dx.astype(jnp.float32).reshape(tok_rows, top_count, piece_width), axis=1
    )
    mixed, grad_tokens, grad_route = (
        lax.psum_scatter(
            mixed_part.astype(jnp.bfloat16), "expert", scatter_dimension=0, tiled=True
        ).astype(jnp.float32),
        lax.psum_scatter(
            dx_part.astype(jnp.bfloat16), "expert", scatter_dimension=0, tiled=True
        ).astype(jnp.float32),
        lax.psum_scatter(
            route_grad.astype(jnp.bfloat16), "expert", scatter_dimension=0, tiled=True
        ).astype(jnp.float32),
    )
    return (
        mixed.astype(jnp.bfloat16),
        grad_tokens.astype(jnp.bfloat16),
        grad_route,
        grad_gate,
        grad_up,
        grad_down,
    )


def solution(mesh):
    return jax.shard_map(
        body,
        mesh=mesh,
        in_specs=(
            P("dp", None),
            P("dp", None),
            P("dp", None),
            P(("dp", "expert"), None, None),
            P(("dp", "expert"), None, None),
            P(("dp", "expert"), None, None),
            P(("dp", "expert"), None),
        ),
        out_specs=(
            P(("dp", "expert"), None),
            P(("dp", "expert"), None),
            P(("dp", "expert"), None),
            P(("dp", "expert"), None, None),
            P(("dp", "expert"), None, None),
            P(("dp", "expert"), None, None),
        ),
        check_vma=False,
    )
```

profile of v0, /device:TPU:1, one launch (start us, length us, event | category | flops | bytes accessed | tf_op | source)
XLA Modules:
  0.0 589.2 jit_solution(7139322173893790338)
XLA Ops:
  14.9 11.8 %scatter_custom_fusion = s32[1153]{0:T(1024)S(1)} fusion(s32[3072]{0:T(1024)S(1)} %bitcast.66, s32[3072]{0:T(1024)S(1)} %iota.13, s32[]{:T(128)} %constant.52.clone.1), kind=kCustom, calls=%fused_computation.64 | custom fusion | bytes 4616 | tf_op jit(solution)/shard_map/scatter | solution.py:49
  26.8 6.0 %gather_fusion = bf16[1152,2048]{1,0:T(8,128)(2,1)} fusion(bf16[512,2048]{1,0:T(8,128)(2,1)S(1)} %copy-done, s32[2048]{0:T(1024)S(1)} %pad_clamp_fusion.1), kind=kCustom, calls=%fused_computation | custom fusion | bytes 9441792 | tf_op jit(solution)/shard_map/gather | solution.py:55
  37.7 7.8 %all-to-all-start = ((bf16[16,72,2048]{2,1,0:T(8,128)(2,1)}), bf16[16,72,2048]{2,1,0:T(8,128)(2,1)}, u32[]{:S(2)}, u32[]{:S(2)}) async-start(bf16[16,72,2048]{2,1,0:T(8,128)(2,1)} %broadcast_select_fusion), calls=%async_computation | async-start | bytes 9437184 | tf_op jit(solution)/shard_map/all_to_all | solution.py:16
  45.9 6.5 %gather_fusion.2 = f32[1152]{0:T(1024)S(1)} fusion(f32[3072]{0:T(1024)S(1)} %reshape.199, s32[2048]{0:T(1024)S(1)} %pad_clamp_fusion), kind=kCustom, calls=%fused_computation.2 | custom fusion | bytes 13824 | tf_op jit(solution)/shard_map/gather | solution.py:81
  53.8 12.5 %gather_fusion.3 = bf16[1152,2048]{1,0:T(8,128)(2,1)} fusion(bf16[512,2048]{1,0:T(8,128)(2,1)} %all-gather.2.cloned.1.call-done, s32[2048]{0:T(1024)S(1)} %pad_clamp_fusion.1), kind=kCustom, calls=%fused_computation.3 | custom fusion | bytes 9441792 | tf_op jit(solution)/shard_map/gather | solution.py:82
  71.7 43.8 %all-to-all-done = bf16[16,72,2048]{2,1,0:T(8,128)(2,1)} async-done(((bf16[16,72,2048]{2,1,0:T(8,128)(2,1)}), bf16[16,72,2048]{2,1,0:T(8,128)(2,1)}, u32[]{:S(2)}, u32[]{:S(2)}) %all-to-all-start) | async-done | bytes 4718624 | tf_op jit(solution)/shard_map/all_to_all | solution.py:16
  120.4 5.7 fusion.10
  126.1 5.6 fusion.14
  131.6 55.8 %all-to-all-done.2 = bf16[16,72,2048]{2,1,0:T(8,128)(2,1)} async-done(((bf16[16,72,2048]{2,1,0:T(8,128)(2,1)}), bf16[16,72,2048]{2,1,0:T(8,128)(2,1)}, u32[]{:S(2)}, u32[]{:S(2)}) %all-to-all-start.2) | async-done | bytes 4718624 | tf_op jit(solution)/shard_map/all_to_all | solution.py:16
  187.5 7.1 %multiply_convert_fusion = (bf16[1152,352]{0,1:T(8,128)(2,1)}, bf16[1152,352]{0,1:T(8,128)(2,1)S(1)}, bf16[1152,352]{0,1:T(8,128)(2,1)S(1)}) fusion(f32[1152,352]{0,1:T(8,128)} %fusion.14, f32[1152,352]{0,1:T(8,128)} %fusion.10, bf16[1152,2048]{1,0:T(8,128)(2,1)} %bitcast.12, bf16[1,352,2048]{2,1,0:T(8,128)(2,1)} %param.12), kind=kOutput, calls=%fused_computation.21 | convolution fusion | flops 1667026944 | bytes 11837440 | tf_op jit(solution)/shard_map/rd,fd->rf/dot_general | solution.py:84
  210.6 56.2 %all-to-all-done.1 = bf16[16,72,2048]{2,1,0:T(8,128)(2,1)} async-done(((bf16[16,72,2048]{2,1,0:T(8,128)(2,1)}), bf16[16,72,2048]{2,1,0:T(8,128)(2,1)}, u32[]{:S(2)}, u32[]{:S(2)}) %all-to-all-start.1) | async-done | bytes 4718624 | tf_op jit(solution)/shard_map/all_to_all | solution.py:22
  272.1 11.3 %mul.105 = f32[512,6,2048]{2,1,0:T(8,128)} broadcast(bf16[512,2048]{1,0:T(8,128)(2,1)S(1)} %copy-done.2), dimensions={0,2} | broadcast | bytes 27262976 | tf_op jit(solution)/shard_map/mul | solution.py:77
  283.4 29.5 %mul.106 = f32[3072,2048]{1,0:T(8,128)} reshape(f32[512,6,2048]{2,1,0:T(8,128)} %mul.105) | data formatting | bytes 50331648 | tf_op jit(solution)/shard_map/mul | solution.py:77
  312.9 26.8 %gather_fusion.1 = bf16[3072,2048]{1,0:T(8,128)(2,1)} fusion(bf16[1152,2048]{1,0:T(8,128)(2,1)} %bitcast.9, s32[3072]{0:T(1024)S(1)} %broadcast_clamp_fusion), kind=kCustom, calls=%fused_computation.1 | custom fusion | bytes 25178112 | tf_op jit(solution)/shard_map/gather | solution.py:71
  339.7 26.8 %gather_fusion.4 = bf16[3072,2048]{1,0:T(8,128)(2,1)} fusion(bf16[1152,2048]{1,0:T(8,128)(2,1)} %bitcast.14, s32[3072]{0:T(1024)S(1)} %broadcast_clamp_fusion), kind=kCustom, calls=%fused_computation.4 | custom fusion | bytes 25178112 | tf_op jit(solution)/shard_map/gather | solution.py:100
  366.5 20.4 %gather.31 = bf16[512,6,2048]{2,1,0:T(8,128)(2,1)} reshape(bf16[3072,2048]{1,0:T(8,128)(2,1)} %gather_fusion.4) | data formatting | bytes 25165824 | tf_op jit(solution)/shard_map/gather | solution.py:100
  386.8 13.1 %multiply_reduce_fusion.1 = bf16[3072]{0:T(1024)(128)(2,1)S(1)} fusion(f32[3072,2048]{1,0:T(8,128)} %mul.106, bf16[3072,2048]{1,0:T(8,128)(2,1)} %gather_fusion.1, pred[3072]{0:T(1024)(128)(4,1)S(1)} %broadcast_compare_fusion), kind=kLoop, calls=%fused_computation.7 | loop fusion | flops 25162752 | bytes 37757952 | tf_op jit(solution)/shard_map/reduce_sum | solution.py:76
  400.9 14.3 %select_reduce_fusion = bf16[512,2048]{1,0:T(8,128)(2,1)} fusion(bf16[512,6,2048]{2,1,0:T(8,128)(2,1)} %gather.31, pred[512,6]{1,0:T(8,128)(4,1)S(1)} %eq.59), kind=kLoop, calls=%fused_computation.8 | loop fusion | flops 11534336 | bytes 14683136 | tf_op jit(solution)/shard_map/reduce_sum | solution.py:101
  415.6 20.4 %gather.26 = bf16[512,6,2048]{2,1,0:T(8,128)(2,1)} reshape(bf16[3072,2048]{1,0:T(8,128)(2,1)} %gather_fusion.1) | data formatting | bytes 25165824 | tf_op jit(solution)/shard_map/gather | solution.py:71
  436.0 20.6 %multiply_reduce_fusion = bf16[512,2048]{1,0:T(8,128)(2,1)} fusion(bf16[512,6,2048]{2,1,0:T(8,128)(2,1)} %gather.26, f32[512,6]{1,0:T(8,128)S(1)} %copy-done.4, pred[512,6]{1,0:T(8,128)(4,1)S(1)} %eq.59), kind=kLoop, calls=%fused_computation.6 | loop fusion | flops 24117248 | bytes 14695424 | tf_op jit(solution)/shard_map/reduce_sum | solution.py:74
  456.6 5.5 fusion.4
  462.2 5.7 fusion.3
  474.7 47.0 %reduce-scatter.6.cloned.1.call-done = bf16[32,2048]{1,0:T(8,128)(2,1)} async-done(((bf16[512,2048]{1,0:T(8,128)(2,1)}), bf16[32,2048]{1,0:T(8,128)(2,1)}) %reduce-scatter.6.cloned.1.call-update) | async-done | bytes 131088 | tf_op jit(solution)/shard_map/reduce_scatter | solution.py:108
  521.7 61.0 %reduce-scatter.4.cloned.1.call-done = bf16[32,2048]{1,0:T(8,128)(2,1)} async-done(((bf16[512,2048]{1,0:T(8,128)(2,1)}), bf16[32,2048]{1,0:T(8,128)(2,1)}) %reduce-scatter.4.cloned.1.call-update) | async-done | bytes 131088 | tf_op jit(solution)/shard_map/reduce_scatter | solution.py:105
  (75 shorter events, 54.0 us)
Async XLA Ops:
  7.2 19.6 %copy-start = (bf16[512,2048]{1,0:T(8,128)(2,1)S(1)}, bf16[512,2048]{1,0:T(8,128)(2,1)}, u32[]{:S(2)}) copy-start(bf16[512,2048]{1,0:T(8,128)(2,1)} %param.7) | copy-start | bytes 6291460
  7.2 46.7 %all-gather.2.cloned.1.call-start = ((), (), s32[]{:S(2)}) async-start(), calls=%async_computation.8 | async-start | bytes 2228224 | tf_op jit(solution)/shard_map/all_gather | solution.py:75
  37.7 7.8 %copy-start.10 = (f32[512,6]{0,1:T(8,128)S(1)}, f32[512,6]{0,1:T(8,128)}, u32[]{:S(2)}) copy-start(f32[512,6]{0,1:T(8,128)} %param.9) | copy-start | bytes 36868
  37.7 77.7 %all-to-all-start = ((bf16[16,72,2048]{2,1,0:T(8,128)(2,1)}), bf16[16,72,2048]{2,1,0:T(8,128)(2,1)}, u32[]{:S(2)}, u32[]{:S(2)}) async-start(bf16[16,72,2048]{2,1,0:T(8,128)(2,1)} %broadcast_select_fusion), calls=%async_computation | async-start | bytes 9437184 | tf_op jit(solution)/shard_map/all_to_all | solution.py:16
  45.7 20.7 %copy-start.3 = (f32[512,6]{1,0:T(8,128)}, f32[512,6]{1,0:T(8,128)S(1)}, u32[]{:S(2)}) copy-start(f32[512,6]{1,0:T(8,128)S(1)} %copy.14) | copy-start | bytes 36868
  71.7 48.7 %copy-start.6 = (bf16[1,352,2048]{2,1,0:T(8,128)(2,1)S(1)}, bf16[1,352,2048]{2,1,0:T(8,128)(2,1)}, u32[]{:S(2)}) copy-start(bf16[1,352,2048]{2,1,0:T(8,128)(2,1)} %param.11) | copy-start | bytes 4325380
  115.4 72.0 %all-to-all-start.2 = ((bf16[16,72,2048]{2,1,0:T(8,128)(2,1)}), bf16[16,72,2048]{2,1,0:T(8,128)(2,1)}, u32[]{:S(2)}, u32[]{:S(2)}) async-start(bf16[16,72,2048]{2,1,0:T(8,128)(2,1)} %fusion), calls=%async_computation.3 | async-start | bytes 9437184 | tf_op jit(solution)/shard_map/all_to_all | solution.py:16
  120.3 5.7 copy-start.5
  187.5 7.1 %copy-start.11 = (bf16[1,352,2048]{2,1,0:T(8,128)(2,1)S(1)}, bf16[1,352,2048]{2,1,0:T(8,128)(2,1)}, u32[]{:S(2)}) copy-start(bf16[1,352,2048]{2,1,0:T(8,128)(2,1)} %param.12) | copy-start | bytes 4325380
  194.6 4.3 copy-start.12
  198.9 67.9 %all-to-all-start.1 = ((bf16[16,72,2048]{2,1,0:T(8,128)(2,1)}), bf16[16,72,2048]{2,1,0:T(8,128)(2,1)}, u32[]{:S(2)}, u32[]{:S(2)}) async-start(bf16[16,72,2048]{2,1,0:T(8,128)(2,1)} %bitcast.61), calls=%async_computation.1 | async-start | bytes 9437184 | tf_op jit(solution)/shard_map/all_to_all | solution.py:22
  203.4 2.7 copy-start.7
  203.5 2.7 copy-start.8
  266.8 5.3 copy-start.2
  266.8 72.9 %all-to-all-start.3 = ((bf16[16,72,2048]{2,1,0:T(8,128)(2,1)}), bf16[16,72,2048]{2,1,0:T(8,128)(2,1)}, u32[]{:S(2)}, u32[]{:S(2)}) async-start(bf16[16,72,2048]{2,1,0:T(8,128)(2,1)} %bitcast.59), calls=%async_computation.4 | async-start | bytes 9437184 | tf_op jit(solution)/shard_map/all_to_all | solution.py:22
  271.5 201.8 %reduce-scatter.8.cloned.1.call-start = ((), (), s32[]{:S(2)}) async-start(), calls=%async_computation.10 | async-start | bytes 139264 | tf_op jit(solution)/shard_map/reduce_scatter | solution.py:111
  400.9 120.8 %reduce-scatter.6.cloned.1.call-start = ((), (), s32[]{:S(2)}) async-start(), calls=%async_computation.9 | async-start | bytes 2228224 | tf_op jit(solution)/shard_map/reduce_scatter | solution.py:108
  415.2 20.7 %copy-start.4 = (f32[512,6]{1,0:T(8,128)S(1)}, f32[512,6]{1,0:T(8,128)}, u32[]{:S(2)}) copy-start(f32[512,6]{1,0:T(8,128)} %copy-done.3) | copy-start | bytes 36868
  415.3 167.4 %reduce-scatter.4.cloned.1.call-start = ((), (), s32[]{:S(2)}) async-start(), calls=%async_computation.7 | async-start | bytes 2228224 | tf_op jit(solution)/shard_map/reduce_scatter | solution.py:105
  435.9 20.6 %copy-start.13 = (bf16[1152,352]{0,1:T(8,128)(2,1)S(1)}, bf16[1152,352]{0,1:T(8,128)(2,1)}, u32[]{:S(2)}) copy-start(bf16[1152,352]{0,1:T(8,128)(2,1)} %copy-done.12) | copy-start | bytes 2433028
  456.6 5.6 copy-start.9
  462.2 120.5 %copy-start.1 = (bf16[512,2048]{1,0:T(8,128)(2,1)S(1)}, bf16[512,2048]{1,0:T(8,128)(2,1)}, u32[]{:S(2)}) copy-start(bf16[512,2048]{1,0:T(8,128)(2,1)} %param.7) | copy-start | bytes 6291460
Sparse Core Ops, SparseCore 0:
  9.8 43.9 all-gather.1
  401.0 59.6 reduce-scatter.7
  464.0 57.6 reduce-scatter.5
  524.8 57.8 reduce-scatter.3
where the time goes:
time: 594 us; the launch traced here: 589 us
  waiting for transfers between devices  266 us (45%)
  local copies, waits for them, and re-layouts  177 us (30%)
  other arithmetic  63.5 us (11%)
  matrix products  46.4 us (8%)
  starting transfers between devices  22.6 us (4%)
  between operations  14.1 us (2%)
    all_to_all x2, waiting for transfers between devices, deliver(): lax.all_to_all(buffer, 'dp', split_axis=0, concat_axis=0, tiled=True)  99.6 us
    reduce_scatter x1, waiting for transfers between devices, body(): lax.psum_scatter(mixed_part.astype(jnp.bfloat16), 'expert', scatter_dimen...  61 us
    all_to_all x2, waiting for transfers between devices, send_back(): lax.all_to_all(rows.reshape(dp_count, slot_count, width), 'dp', split_axi...  56.3 us
    gather x2, local copies, waits for them, and re-layouts, body(): returned[safe_target]  47.2 us
    gather x2, local copies, waits for them, and re-layouts, body(): dx_back[safe_target]  47.1 us
    reduce_scatter x1, waiting for transfers between devices, body(): lax.psum_scatter(dx_part.astype(jnp.bfloat16), 'expert', scatter_dimensio...  47 us
    mul x2, local copies, waits for them, and re-layouts, body(): route_part.reshape(tok_rows, top_count, piece_width).astype(jnp.float32)  40.8 us
    reduce_sum x1, other arithmetic, body(): jnp.sum(weighted.reshape(tok_rows, top_count, piece_width), axis=1)  20.6 us
  transfers between devices with their start and end apart: 8, of which 6 were waited for; matrix products, arithmetic and copies ran while one was open for 36% of the time, Pallas kernels for 0%

commit v1 on v0

v1 whole, which is shorter than its diff:
```python
import jax
import jax.numpy as jnp
from jax import lax
from jax.experimental import pallas as pl
from jax.experimental.pallas import tpu as pltpu
from jax.sharding import PartitionSpec as P

MESH = pl.DeviceIdType.MESH
F32 = jnp.float32
BF16 = jnp.bfloat16

TOK = 512
D = 2048
HALF = 1024
FF = 352
TOP = 6
CAP = 72
T8 = CAP // 8
NDP = 16
NEX = 16
BLK = TOK // NEX
ROWS = 4 * CAP
COLS = 512


def rows_of(ref_value):
    return ref_value.reshape(-1, ref_value.shape[-1])


def nt(a, b):
    return lax.dot_general(a, b, (((1,), (1,)), ((), ())), preferred_element_type=F32)


def tn(a, b):
    return lax.dot_general(a, b, (((0,), (0,)), ((), ())), preferred_element_type=F32)


def nn(a, b):
    return jnp.dot(a, b, preferred_element_type=F32)


def kernel(
    tok_hbm, routes_ref, weight_ref, wg_hbm, wu_hbm, wd_hbm, g_hbm,
    mixed_ref, dx_ref, grw_ref, gg_hbm, gu_hbm, gd_hbm,
    tok, gloc, gall, wg, wu, wd, hits, rank, wtok, sel,
    xs, xr, gs, gr, ws, wr, vs, vret,
    yo, ypo, ypi, yret, do, dpo, dpi, dret,
    gate_s, up_s, hwt, dgt, dut,
    mst, mrecv, dst_, drecv, rst, rrecv, gg, gu, gd,
    in_sem, out_sem, sgz, rgz, sx, rx, sxf, rxf, sw, rw, sg, rg, sgf, rgf,
    syp, ryp, sy, ry, sdp, rdp, sd, rd, sv, rv, sm, rm, sz, rz, sr, rr,
):
    dp = lax.axis_index("dp")
    ex = lax.axis_index("expert")
    px, py = dp % 4, dp // 4
    core = ex % 2
    other = 1 - core
    group = ex // 4
    partner = (dp, ex + 1 - 2 * core)

    def gray(v):
        return v + (v // 2) * (1 - 2 * (v % 2))

    def to_dp(k):
        return ((py + gray(k // 4)) % 4) * 4 + (px + gray(k % 4)) % 4

    def from_dp(k):
        return ((py + 4 - gray(k // 4)) % 4) * 4 + (px + 4 - gray(k % 4)) % 4

    def to_ex(m):
        return (ex + m) % NEX

    def remote(src, dst, ssem, rsem, where):
        return pltpu.make_async_remote_copy(
            src_ref=src, dst_ref=dst, send_sem=ssem, recv_sem=rsem,
            device_id=where, device_id_type=MESH,
        )

    def cp_gz(m):
        e2 = to_ex(m)
        return remote(gloc.at[e2 % 2], gall.at[ex], sgz.at[m], rgz.at[m], (dp, e2))

    def cp_x(k):
        return remote(xs.at[k], xr.at[core, k], sx.at[k], rx.at[k], (to_dp(k), ex))

    def cp_xf(q):
        half = xr.at[core, pl.ds(q * 4, 4)]
        return remote(half, half, sxf.at[q], rxf.at[q], partner)

    def cp_w(k):
        return remote(ws.at[k], wr.at[k], sw.at[k], rw.at[k], (to_dp(k), ex))

    def cp_g(k):
        return remote(gs.at[k], gr.at[core, k], sg.at[k], rg.at[k], (to_dp(k), ex))

    def cp_gf(q):
        half = gr.at[core, pl.ds(q * 4, 4)]
        return remote(half, half, sgf.at[q], rgf.at[q], partner)

    def cp_yp(q):
        at = pl.ds(q * 4, 4)
        return remote(ypo.at[at], ypi.at[at], syp.at[q], ryp.at[q], partner)

    def cp_y(k):
        return remote(yo.at[k], yret.at[k], sy.at[k], ry.at[k], (from_dp(k), ex))

    def cp_dp(q):
        at = pl.ds(q * 4, 4)
        return remote(dpo.at[at], dpi.at[at], sdp.at[q], rdp.at[q], partner)

    def cp_d(k):
        return remote(do.at[k], dret.at[k], sd.at[k], rd.at[k], (from_dp(k), ex))

    def cp_v(k):
        return remote(vs.at[k], vret.at[k], sv.at[k], rv.at[k], (from_dp(k), ex))

    def cp_m(m):
        e2 = to_ex(m)
        return remote(mst.at[e2], mrecv.at[ex], sm.at[m], rm.at[m], (dp, e2))

    def cp_z(m):
        e2 = to_ex(m)
        return remote(dst_.at[e2], drecv.at[ex], sz.at[m], rz.at[m], (dp, e2))

    def cp_r(m):
        e2 = to_ex(m)
        return remote(rst.at[e2 // 4], rrecv.at[ex], sr.at[m], rr.at[m], (dp, e2))

    def loop(lo, hi, fn):
        def step(i, carry):
            fn(i)
            return carry

        lax.fori_loop(lo, hi, step, 0)

    loads = [
        pltpu.make_async_copy(g_hbm.at[:, pl.ds(0, HALF)], gloc.at[0], in_sem.at[0]),
        pltpu.make_async_copy(g_hbm.at[:, pl.ds(HALF, HALF)], gloc.at[1], in_sem.at[1]),
        pltpu.make_async_copy(tok_hbm.at[:, pl.ds(pl.multiple_of(core * HALF, HALF), HALF)], tok, in_sem.at[2]),
        pltpu.make_async_copy(wg_hbm.at[0], wg, in_sem.at[3]),
        pltpu.make_async_copy(wu_hbm.at[0], wu, in_sem.at[4]),
        pltpu.make_async_copy(wd_hbm.at[0], wd, in_sem.at[5]),
    ]
    for load in loads:
        load.start()

    barrier = pltpu.get_barrier_semaphore()

    def greet(k):
        pl.semaphore_signal(barrier, inc=1, device_id=(to_dp(k), ex), device_id_type=MESH)
        pl.semaphore_signal(barrier, inc=1, device_id=(dp, to_ex(k)), device_id_type=MESH)

    loop(1, NDP, greet)

    def find(k):
        named = routes_ref[...] == to_dp(k) * 4 + group
        hits[pl.ds(k, 1), :] = jnp.sum(named.astype(F32), axis=0, keepdims=True)
        wtok[pl.ds(k, 1), :] = jnp.sum(jnp.where(named, weight_ref[...], 0.0), axis=0, keepdims=True)

    loop(0, NDP, find)
    before = lax.broadcasted_iota(jnp.int32, (TOK, TOK), 0) < lax.broadcasted_iota(jnp.int32, (TOK, TOK), 1)
    ranks = nn(hits[...].astype(BF16), before.astype(F32).astype(BF16))
    rank[...] = jnp.where(hits[...] > 0.5, ranks, -1.0)

    loads[0].wait()
    loads[1].wait()
    pl.semaphore_wait(barrier, 2 * (NDP - 1))
    loop(1, NEX, lambda m: cp_gz(m).start())
    gall[pl.ds(ex, 1)] = gloc[pl.ds(core, 1)]
    loads[2].wait()

    eye = (
        lax.broadcasted_iota(jnp.int32, (CAP, 128), 0) == lax.broadcasted_iota(jnp.int32, (CAP, 128), 1)
    ).astype(F32)

    def to_row(col):
        return jnp.broadcast_to(jnp.sum(eye * col, axis=0, keepdims=True), (8, 128))

    def to_col(row):
        return jnp.sum(eye * row, axis=1, keepdims=True)

    def pick(k):
        slot = lax.broadcasted_iota(jnp.int32, (CAP, TOK), 0).astype(F32)
        hot = (slot == rank[pl.ds(k, 1), :]).astype(F32)
        s = hot.astype(BF16)
        sel[pl.ds(k, 1)] = s.reshape(1, T8, 8, TOK)
        x = nn(s, tok[...]).astype(BF16).reshape(1, T8, 8, HALF)
        w = jnp.sum(hot * wtok[pl.ds(k, 1), :], axis=1, keepdims=True)
        return x, to_row(w)[None]

    def send_x(k):
        x, w = pick(k)
        xs[pl.ds(k, 1)] = x
        ws[pl.ds(k, 1)] = w
        cp_x(k).start()
        cp_w(k).start()

    x0, w0 = pick(0)
    xr[pl.ds(core, 1), 0:1] = x0[None]
    wr[0:1] = w0
    loop(1, NDP, send_x)

    loop(1, NEX, lambda m: cp_gz(m).wait_recv())

    def g_chunk(k):
        return nn(rows_of(sel[pl.ds(k, 1)]), rows_of(gall[...])).astype(BF16).reshape(1, T8, 8, HALF)

    def send_g(k):
        gs[pl.ds(k, 1)] = g_chunk(k)
        cp_g(k).start()

    def got_x(k):
        cp_x(k).wait_recv()
        cp_w(k).wait_recv()

    def pass_x(q):
        loop(jnp.maximum(q * 4, 1), q * 4 + 4, got_x)
        cp_xf(q).start()
        loop(jnp.maximum(q * 4, 1), q * 4 + 4, send_g)

    gr[pl.ds(core, 1), 0:1] = g_chunk(0)[None]
    for load in loads[3:]:
        load.wait()

    def weight_col(q):
        return jnp.concatenate([to_col(wr[pl.ds(q * 4 + r, 1)][0, 0:1]) for r in range(4)], axis=0)

    def forward(q):
        cp_xf(q).wait_recv()
        at = pl.ds(q * 4, 4)
        x0 = rows_of(xr[0, at])
        x1 = rows_of(xr[1, at])
        gate = nt(x0, wg[:, :HALF]) + nt(x1, wg[:, HALF:])
        up = nt(x0, wu[:, :HALF]) + nt(x1, wu[:, HALF:])
        gate_s[q] = gate
        up_s[q] = up
        hidden = gate * jax.nn.sigmoid(gate) * up
        hw = (weight_col(q) * hidden).astype(BF16)
        hwt[q] = hw.T
        send = pl.multiple_of(other * HALF, HALF)
        keep = pl.multiple_of(core * HALF, HALF)
        ypo[at] = nn(hw, wd[:, pl.ds(send, HALF)]).astype(BF16).reshape(4, T8, 8, HALF)
        cp_yp(q).start()
        yo[at] = nn(hw, wd[:, pl.ds(keep, HALF)]).astype(BF16).reshape(4, T8, 8, HALF)

    def return_y(q):
        cp_yp(q).wait_recv()
        at = pl.ds(q * 4, 4)
        yo[at] = (yo[at].astype(F32) + ypi[at].astype(F32)).astype(BF16)
        loop(jnp.maximum(q * 4, 1), q * 4 + 4, lambda k: cp_y(k).start())

    def forward_step(q):
        @pl.when(q < 4)
        def _():
            pass_x(q)

        @pl.when((q >= 1) & (q < 5))
        def _():
            forward(q - 1)

        @pl.when(q >= 2)
        def _():
            return_y(q - 2)

    loop(0, 6, forward_step)
    yret[0:1] = yo[0:1]

    def pass_g(q):
        loop(jnp.maximum(q * 4, 1), q * 4 + 4, lambda k: cp_g(k).wait_recv())
        cp_gf(q).start()

    def backward(q):
        cp_gf(q).wait_recv()
        at = pl.ds(q * 4, 4)
        dh = nt(rows_of(gr[0, at]), wd[:, :HALF]) + nt(rows_of(gr[1, at]), wd[:, HALF:])
        gate = gate_s[q]
        up = up_s[q]
        sigma = jax.nn.sigmoid(gate)
        silu = gate * sigma
        slope = sigma * (1.0 + gate * (1.0 - sigma))
        dot = jnp.sum(silu * up * dh, axis=1, keepdims=True)
        for r in range(4):
            vs[pl.ds(q * 4 + r, 1)] = to_row(dot[r * CAP : (r + 1) * CAP])[None]
        loop(jnp.maximum(q * 4, 1), q * 4 + 4, lambda k: cp_v(k).start())
        dh = weight_col(q) * dh
        dg = (dh * up * slope).astype(BF16)
        du = (dh * silu).astype(BF16)
        dgt[q] = dg.T
        dut[q] = du.T
        send = pl.ds(pl.multiple_of(other * HALF, HALF), HALF)
        keep = pl.ds(pl.multiple_of(core * HALF, HALF), HALF)
        dpo[at] = (nn(dg, wg[:, send]) + nn(du, wu[:, send])).astype(BF16).reshape(4, T8, 8, HALF)
        cp_dp(q).start()
        do[at] = (nn(dg, wg[:, keep]) + nn(du, wu[:, keep])).astype(BF16).reshape(4, T8, 8, HALF)

    def return_d(q):
        cp_dp(q).wait_recv()
        at = pl.ds(q * 4, 4)
        do[at] = (do[at].astype(F32) + dpi[at].astype(F32)).astype(BF16)
        loop(jnp.maximum(q * 4, 1), q * 4 + 4, lambda k: cp_d(k).start())

    def backward_step(q):
        @pl.when(q < 4)
        def _():
            pass_g(q)

        @pl.when((q >= 1) & (q < 5))
        def _():
            backward(q - 1)

        @pl.when(q >= 2)
        def _():
            return_d(q - 2)

    loop(0, 6, backward_step)
    dret[0:1] = do[0:1]
    vret[0:1] = vs[0:1]

    def combine(back, stage):
        def part(n):
            cols = pl.ds(pl.multiple_of(n * COLS, COLS), COLS)
            total = tn(rows_of(sel[0:4]), rows_of(back[0:4, :, :, cols]))
            for q in range(1, 4):
                at = slice(q * 4, q * 4 + 4)
                total += tn(rows_of(sel[at]), rows_of(back[at, :, :, cols]))
            stage[:, :, cols] = total.astype(BF16).reshape(NEX, BLK, COLS)

        loop(0, HALF // COLS, part)

    loop(1, NDP, lambda k: cp_y(k).wait_recv())
    combine(yret, mst)
    loop(1, NEX, lambda m: cp_m(m).start())
    mrecv[pl.ds(ex, 1)] = mst[pl.ds(ex, 1)]

    def grads(n):
        h = n // (HALF // COLS)
        cols = pl.ds(pl.multiple_of((n % (HALF // COLS)) * COLS, COLS), COLS)
        outs = pl.ds(pl.multiple_of(n * COLS, COLS), COLS)

        def total(left, right):
            acc = nn(left[0], rows_of(right[h, 0:4, :, :, cols]))
            for q in range(1, 4):
                acc += nn(left[q], rows_of(right[h, q * 4 : q * 4 + 4, :, :, cols]))
            return acc.astype(BF16)

        gd[:, outs] = total(hwt, gr)
        gg[:, outs] = total(dgt, xr)
        gu[:, outs] = total(dut, xr)

    loop(0, D // COLS, grads)
    stores = [
        pltpu.make_async_copy(gg, gg_hbm.at[0], out_sem.at[0]),
        pltpu.make_async_copy(gu, gu_hbm.at[0], out_sem.at[1]),
        pltpu.make_async_copy(gd, gd_hbm.at[0], out_sem.at[2]),
    ]
    for store in stores:
        store.start()

    rst[...] = jnp.zeros_like(rst)
    loop(1, NDP, lambda k: cp_v(k).wait_recv())

    def route_grad(k):
        col = to_col(vret[pl.ds(k, 1)][0, 0:1])
        row = jnp.sum(rows_of(sel[pl.ds(k, 1)]).astype(F32) * col, axis=0, keepdims=True)
        add = jnp.where(routes_ref[...] == to_dp(k) * 4 + group, row, 0.0)
        for b in range(4):
            rst[b] += add[:, b * 128 : (b + 1) * 128]

    loop(0, NDP, route_grad)
    loop(1, NEX, lambda m: cp_r(m).start())
    rrecv[pl.ds(ex, 1)] = rst[pl.ds(group, 1)]

    loop(1, NDP, lambda k: cp_d(k).wait_recv())
    combine(dret, dst_)
    loop(1, NEX, lambda m: cp_z(m).start())
    drecv[pl.ds(ex, 1)] = dst_[pl.ds(ex, 1)]

    def finish(recv, out):
        for h in range(2):
            total = recv[h].astype(F32)
            for zz in range(1, 8):
                total += recv[zz * 2 + h].astype(F32)
            out[:, h * HALF : (h + 1) * HALF] = total.astype(BF16)

    loop(1, NEX, lambda m: cp_m(m).wait_recv())
    finish(mrecv, mixed_ref)
    loop(1, NEX, lambda m: cp_r(m).wait_recv())
    route_total = jnp.sum(rrecv[...], axis=0)
    mine = (
        lax.broadcasted_iota(jnp.int32, (BLK, 128), 1)
        == lax.broadcasted_iota(jnp.int32, (BLK, 128), 0) + (ex % 4) * BLK
    ).astype(F32)
    lane = lax.broadcasted_iota(jnp.int32, (BLK, 128), 1)
    placed = jnp.zeros((BLK, 128), F32)
    for kk in range(TOP):
        col = jnp.sum(mine * route_total[kk : kk + 1], axis=1, keepdims=True)
        placed = jnp.where(lane == kk, col, placed)
    grw_ref[...] = placed[:, :TOP]
    loop(1, NEX, lambda m: cp_z(m).wait_recv())
    finish(drecv, dx_ref)

    def sent_dp(k):
        cp_x(k).wait_send()
        cp_w(k).wait_send()
        cp_g(k).wait_send()
        cp_y(k).wait_send()
        cp_d(k).wait_send()
        cp_v(k).wait_send()
        cp_gz(k).wait_send()
        cp_m(k).wait_send()
        cp_z(k).wait_send()
        cp_r(k).wait_send()

    loop(1, NDP, sent_dp)

    def sent_q(q):
        cp_xf(q).wait_send()
        cp_gf(q).wait_send()
        cp_yp(q).wait_send()
        cp_dp(q).wait_send()

    loop(0, 4, sent_q)
    for store in stores:
        store.wait()


def body(tokens, routes, route_weight, w_gate, w_up, w_down, grad_out):
    routes_t = jnp.pad(routes.T, ((0, 2), (0, 0)), constant_values=-1)
    weight_t = jnp.pad(route_weight.T, ((0, 2), (0, 0)))
    any_ = pl.BlockSpec(memory_space=pl.ANY)
    vmem = pl.BlockSpec(memory_space=pltpu.VMEM)
    chunk = (NDP, T8, 8, HALF)
    dma = pltpu.SemaphoreType.DMA
    V = pltpu.VMEM
    mixed, dx, grw, gg, gu, gd = pl.pallas_call(
        kernel,
        out_shape=(
            jax.ShapeDtypeStruct((BLK, D), BF16),
            jax.ShapeDtypeStruct((BLK, D), BF16),
            jax.ShapeDtypeStruct((BLK, TOP), F32),
            jax.ShapeDtypeStruct((1, FF, D), BF16),
            jax.ShapeDtypeStruct((1, FF, D), BF16),
            jax.ShapeDtypeStruct((1, FF, D), BF16),
        ),
        in_specs=[any_, vmem, vmem, any_, any_, any_, any_],
        out_specs=(vmem, vmem, vmem, any_, any_, any_),
        scratch_shapes=[
            V((TOK, HALF), BF16), V((2, BLK, HALF), BF16), V((NEX, BLK, HALF), BF16),
            V((FF, D), BF16), V((FF, D), BF16), V((FF, D), BF16),
            V((NDP, TOK), F32), V((NDP, TOK), F32), V((NDP, TOK), F32), V((NDP, T8, 8, TOK), BF16),
            V(chunk, BF16), V((2,) + chunk, BF16), V(chunk, BF16), V((2,) + chunk, BF16),
            V((NDP, 8, 128), F32), V((NDP, 8, 128), F32), V((NDP, 8, 128), F32), V((NDP, 8, 128), F32),
            V(chunk, BF16), V(chunk, BF16), V(chunk, BF16), V(chunk, BF16),
            V(chunk, BF16), V(chunk, BF16), V(chunk, BF16), V(chunk, BF16),
            V((4, ROWS, FF), F32), V((4, ROWS, FF), F32),
            V((4, FF, ROWS), BF16), V((4, FF, ROWS), BF16), V((4, FF, ROWS), BF16),
            V((NEX, BLK, HALF), BF16), V((NEX, BLK, HALF), BF16), V((NEX, BLK, HALF), BF16), V((NEX, BLK, HALF), BF16),
            V((4, 8, 128), F32), V((NEX, 8, 128), F32),
            V((FF, D), BF16), V((FF, D), BF16), V((FF, D), BF16),
            dma((6,)), dma((3,)),
            dma((16,)), dma((16,)), dma((16,)), dma((16,)), dma((4,)), dma((4,)),
            dma((16,)), dma((16,)), dma((16,)), dma((16,)), dma((4,)), dma((4,)),
            dma((4,)), dma((4,)), dma((16,)), dma((16,)), dma((4,)), dma((4,)),
            dma((16,)), dma((16,)), dma((16,)), dma((16,)),
            dma((16,)), dma((16,)), dma((16,)), dma((16,)), dma((16,)), dma((16,)),
        ],
        compiler_params=pltpu.CompilerParams(
            collective_id=0, has_side_effects=True, vmem_limit_bytes=63_000_000
        ),
    )(tokens, routes_t, weight_t, w_gate, w_up, w_down, grad_out)
    return mixed, dx, grw, gg, gu, gd


def solution(mesh):
    rows = P(("dp", "expert"), None)
    block = P(("dp", "expert"), None, None)
    return jax.shard_map(
        body,
        mesh=mesh,
        in_specs=(P("dp", None), P("dp", None), P("dp", None), block, block, block, rows),
        out_specs=(rows, rows, rows, block, block, block),
        check_vma=False,
    )
```

time: 594 us -> 189 us (0.32)
  the two profiles are of different devices: /device:TPU:1 before, /device:TPU:193 now
where the time goes in v1:
time: 189 us; the launch traced here: 188 us
  Pallas kernels  175 us (93%)
  local copies, waits for them, and re-layouts  12.9 us (7%)
    pallas_call x1, Pallas kernels, body(): pl.pallas_call(kernel, out_shape=(jax.ShapeDtypeStruct((BLK, D), BF16), j...  175 us
    unnamed x9, local copies, waits for them, and re-layouts  8.85 us

profile of v1, /device:TPU:193, one launch (start us, length us, event | category | flops | bytes accessed | tf_op | source)
XLA Modules:
  0.0 188.3 jit_solution(17431277179891944626)
XLA Ops:
  0.6 1.3 pad.8.routes_ref
  2.0 1.3 pad.9.weight_ref
  3.3 174.8 %shard_map.118 = (bf16[32,2048]{1,0:T(8,128)(2,1)}, bf16[32,2048]{1,0:T(8,128)(2,1)}, f32[32,6]{1,0:T(8,128)}, bf16[1,352,2048]{2,1,0:T(8,128)(2,1)}, bf16[1,352...) custom-call(bf16[512,2048]{1,0:T(8,128)(2,1)} %tok_hbm.1, s32[8,512]{1,0:T(8,128)} %pad.8.routes_ref, ...), custom_call_target="tpu_custom_call" | custom-call | tf_op jit(solution)/shard_map/pallas_call | solution.py:435
  178.1 1.4 copy.13
  179.4 1.6 copy.19
  181.0 1.6 copy.20
  182.6 0.0 copy-start.1
  182.6 2.7 %copy.21 = bf16[1,352,2048]{2,1,0:T(8,128)(2,1)} copy(bf16[1,352,2048]{2,1,0:T(8,128)(2,1)} %get-tuple-element.21) | data formatting | bytes 2883584
  185.3 0.0 copy-done.1
  185.3 0.0 copy-start
  185.3 1.1 copy.22
  186.4 0.8 copy-done
  187.2 1.1 copy.23
Async XLA Ops:
  182.6 2.7 %copy-start.1 = (bf16[1,352,2048]{2,1,0:T(8,128)(2,1)S(1)}, bf16[1,352,2048]{2,1,0:T(8,128)(2,1)}, u32[]{:S(2)}) copy-start(bf16[1,352,2048]{2,1,0:T(8,128)(2,1)} %get-tuple-element.22) | copy-start | bytes 4325380
  185.3 1.9 %copy-start = (bf16[1,352,2048]{2,1,0:T(8,128)(2,1)S(1)}, bf16[1,352,2048]{2,1,0:T(8,128)(2,1)}, u32[]{:S(2)}) copy-start(bf16[1,352,2048]{2,1,0:T(8,128)(2,1)} %get-tuple-element.23) | copy-start | bytes 4325380

commit v2 on v1

v2 whole, which is shorter than its diff:
```python
import jax
import jax.numpy as jnp
from jax import lax
from jax.experimental import pallas as pl
from jax.experimental.pallas import tpu as pltpu
from jax.sharding import PartitionSpec as P

MESH = pl.DeviceIdType.MESH
F32 = jnp.float32
BF16 = jnp.bfloat16

TOK = 512
D = 2048
HALF = 1024
FF = 352
TOP = 6
CAP = 72
T8 = CAP // 8
NDP = 16
NEX = 16
BLK = TOK // NEX
ROWS = 4 * CAP
COLS = 512
QUART = 512
PH = 4
PCOL = HALF // PH


def rows_of(ref_value):
    return ref_value.reshape(-1, ref_value.shape[-1])


def nt(a, b):
    return lax.dot_general(a, b, (((1,), (1,)), ((), ())), preferred_element_type=F32)


def tn(a, b):
    return lax.dot_general(a, b, (((0,), (0,)), ((), ())), preferred_element_type=F32)


def nn(a, b):
    return jnp.dot(a, b, preferred_element_type=F32)


def kernel(
    tok_hbm, routes_ref, weight_ref, wg_hbm, wu_hbm, wd_hbm, g_hbm,
    mixed_ref, dx_ref, grw_ref, gg_hbm, gu_hbm, gd_hbm,
    tok, gloc, gall, wg, wu, wd, hits, rank, wtok, sel, selt,
    xs, xr, gs, gr, ws, wr, vs, vret,
    yo, ypi, yzo, yzi, yq, yret, do, dpo, dpi, dret,
    gate_s, up_s, hwt, dgt, dut, dgs, dus,
    mst, mrecv, dst_, drecv, rst, rrecv, gg, gu, gd,
    in_sem, out_sem, sgz, rgz, sx, rx, sxf, rxf, sw, rw, sg, rg, sgf, rgf,
    syp, ryp, syz, ryz, sy, ry, sdp, rdp, sd, rd, sv, rv, sm, rm, sz, rz, sr, rr,
):
    dp = lax.axis_index("dp")
    ex = lax.axis_index("expert")
    px, py = dp % 4, dp // 4
    core = ex % 2
    other = 1 - core
    group = ex // 4
    partner = (dp, ex + 1 - 2 * core)
    odd = (ex // 2) % 2
    across = (dp, ex + 2 - 4 * odd)

    def gray(v):
        return v + (v // 2) * (1 - 2 * (v % 2))

    def to_dp(k):
        return ((py + gray(k // 4)) % 4) * 4 + (px + gray(k % 4)) % 4

    def from_dp(k):
        return ((py + 4 - gray(k // 4)) % 4) * 4 + (px + 4 - gray(k % 4)) % 4

    def to_ex(m):
        return (ex + m) % NEX

    def remote(src, dst, ssem, rsem, where):
        return pltpu.make_async_remote_copy(
            src_ref=src, dst_ref=dst, send_sem=ssem, recv_sem=rsem,
            device_id=where, device_id_type=MESH,
        )

    def cp_gz(m):
        e2 = to_ex(m)
        return remote(gloc.at[e2 % 2], gall.at[ex], sgz.at[0], rgz.at[0], (dp, e2))

    def many_gz():
        return remote(gall.at[pl.ds(0, 15)], gall.at[pl.ds(0, 15)], sgz.at[0], rgz.at[0], partner)

    def many_x(k, n):
        at = pl.ds(k, n)
        return remote(xs.at[at], xr.at[core, at], sx.at[k // 4], rx.at[k // 4], (to_dp(k), ex))

    def cp_xf(q):
        half = xr.at[core, pl.ds(q * 4, 4)]
        return remote(half, half, sxf.at[0], rxf.at[q], partner)

    def many_w(k, n):
        at = pl.ds(k, n)
        return remote(ws.at[at], wr.at[at], sw.at[0], rw.at[k // 4], (to_dp(k), ex))

    def many_g(k, n):
        at = pl.ds(k, n)
        return remote(gs.at[at], gr.at[core, at], sg.at[0], rg.at[k // 4], (to_dp(k), ex))

    def cp_gf(q):
        half = gr.at[core, pl.ds(q * 4, 4)]
        return remote(half, half, sgf.at[0], rgf.at[q], partner)

    def many_yp(q, n):
        at = pl.ds(q * 4, 4 * n)
        return remote(xs.at[at], ypi.at[at], syp.at[0], ryp.at[q], partner)

    def many_yz(q, n):
        at = pl.ds(q * 4, 4 * n)
        return remote(yzo.at[at], yzi.at[at], syz.at[0], ryz.at[q], across)

    def many_y(k, n):
        at = pl.ds(k, n)
        return remote(yq.at[at], yret.at[at], sy.at[0], ry.at[0], (from_dp(k), ex))

    def many_dp(i, n):
        at = pl.ds(i * 4, 4 * n)
        return remote(dpo.at[at], dpi.at[at], sdp.at[0], rdp.at[i], partner)

    def many_d(p, k, n):
        at = pl.ds(p * NDP + k, n)
        return remote(do.at[at], dret.at[at], sd.at[p], rd.at[p], (from_dp(k), ex))

    def many_v(k, n):
        at = pl.ds(k, n)
        return remote(vs.at[at], vret.at[at], sv.at[0], rv.at[0], (from_dp(k), ex))

    def cp_m(m):
        e2 = to_ex(m)
        return remote(mst.at[e2], mrecv.at[ex], sm.at[0], rm.at[0], (dp, e2))

    def many_m():
        return remote(mst.at[pl.ds(0, 15)], mrecv.at[pl.ds(0, 15)], sm.at[0], rm.at[0], partner)

    def cp_z(p, m):
        e2 = to_ex(m)
        return remote(dst_.at[p, e2], drecv.at[p, ex], sz.at[p], rz.at[p], (dp, e2))

    def many_z(p):
        at = pl.ds(0, 15)
        return remote(dst_.at[p, at], drecv.at[p, at], sz.at[p], rz.at[p], partner)

    def cp_r(m):
        e2 = to_ex(m)
        return remote(rst.at[e2 // 4], rrecv.at[ex], sr.at[0], rr.at[0], (dp, e2))

    def many_r():
        at = pl.ds(0, 15)
        return remote(rrecv.at[at], rrecv.at[at], sr.at[0], rr.at[0], partner)

    def by_group(q, fn):
        @pl.when(q == 0)
        def _():
            fn(1, 3)

        @pl.when(q > 0)
        def _():
            fn(q * 4, 4)

    def loop(lo, hi, fn):
        def step(i, carry):
            fn(i)
            return carry

        lax.fori_loop(lo, hi, step, 0)

    loads = [
        pltpu.make_async_copy(g_hbm.at[:, pl.ds(0, HALF)], gloc.at[0], in_sem.at[0]),
        pltpu.make_async_copy(g_hbm.at[:, pl.ds(HALF, HALF)], gloc.at[1], in_sem.at[1]),
        pltpu.make_async_copy(tok_hbm.at[:, pl.ds(pl.multiple_of(core * HALF, HALF), HALF)], tok, in_sem.at[2]),
        pltpu.make_async_copy(wg_hbm.at[0], wg, in_sem.at[3]),
        pltpu.make_async_copy(wu_hbm.at[0], wu, in_sem.at[4]),
        pltpu.make_async_copy(wd_hbm.at[0], wd, in_sem.at[5]),
    ]
    for load in loads:
        load.start()

    barrier = pltpu.get_barrier_semaphore()

    def greet(k):
        pl.semaphore_signal(barrier, inc=1, device_id=(to_dp(k), ex), device_id_type=MESH)
        pl.semaphore_signal(barrier, inc=1, device_id=(dp, to_ex(k)), device_id_type=MESH)

    loop(1, NDP, greet)

    def find(k):
        named = routes_ref[...] == to_dp(k) * 4 + group
        hits[pl.ds(k, 1), :] = jnp.sum(named.astype(F32), axis=0, keepdims=True)
        wtok[pl.ds(k, 1), :] = jnp.sum(jnp.where(named, weight_ref[...], 0.0), axis=0, keepdims=True)

    loop(0, NDP, find)
    before = lax.broadcasted_iota(jnp.int32, (TOK, TOK), 0) < lax.broadcasted_iota(jnp.int32, (TOK, TOK), 1)
    ranks = nn(hits[...].astype(BF16), before.astype(F32).astype(BF16))
    rank[...] = jnp.where(hits[...] > 0.5, ranks, -1.0)

    loads[0].wait()
    loads[1].wait()
    pl.semaphore_wait(barrier, 2 * (NDP - 1))
    loop(1, NEX, lambda m: cp_gz(m).start())
    gall[pl.ds(ex, 1)] = gloc[pl.ds(core, 1)]
    loads[2].wait()

    eye = (
        lax.broadcasted_iota(jnp.int32, (CAP, 128), 0) == lax.broadcasted_iota(jnp.int32, (CAP, 128), 1)
    ).astype(F32)

    def to_row(col):
        return jnp.broadcast_to(jnp.sum(eye * col, axis=0, keepdims=True), (8, 128))

    def to_col(row):
        return jnp.sum(eye * row, axis=1, keepdims=True)

    slot = lax.broadcasted_iota(jnp.int32, (CAP, TOK), 0).astype(F32)

    def send_x(q):
        at = pl.ds(q * 4, 4)
        hot = []
        for r in range(4):
            k = q * 4 + r
            one = (slot == rank[pl.ds(k, 1), :]).astype(F32)
            w = jnp.sum(one * wtok[pl.ds(k, 1), :], axis=1, keepdims=True)
            ws[pl.ds(k, 1)] = to_row(w)[None]
            hot.append(one)
        s = jnp.concatenate(hot, axis=0).astype(BF16)
        sel[at] = s.reshape(4, T8, 8, TOK)
        xs[at] = nn(s, tok[...]).astype(BF16).reshape(4, T8, 8, HALF)

        def go(k):
            many_x(k, 1).start()
            many_w(k, 1).start()

        loop(jnp.maximum(q * 4, 1), q * 4 + 4, go)
        selt[q] = s.T

    loop(0, 4, send_x)
    xr[pl.ds(core, 1), 0:1] = xs[0:1][None]
    wr[0:1] = ws[0:1]

    many_gz().wait_recv()

    def send_g(q):
        at = pl.ds(q * 4, 4)
        gs[at] = nn(rows_of(sel[at]), rows_of(gall[...])).astype(BF16).reshape(4, T8, 8, HALF)
        loop(jnp.maximum(q * 4, 1), q * 4 + 4, lambda k: many_g(k, 1).start())

    def pass_x(q):
        by_group(q, lambda k, n: many_x(k, n).wait_recv())
        by_group(q, lambda k, n: many_w(k, n).wait_recv())
        cp_xf(q).start()

    loop(0, 4, send_g)
    gr[pl.ds(core, 1), 0:1] = gs[0:1][None]
    for load in loads[3:]:
        load.wait()

    def weight_col(q):
        return jnp.concatenate([to_col(wr[pl.ds(q * 4 + r, 1)][0, 0:1]) for r in range(4)], axis=0)

    def forward(q):
        cp_xf(q).wait_recv()
        at = pl.ds(q * 4, 4)
        x0 = rows_of(xr[0, at])
        x1 = rows_of(xr[1, at])
        gate = nt(x0, wg[:, :HALF]) + nt(x1, wg[:, HALF:])
        up = nt(x0, wu[:, :HALF]) + nt(x1, wu[:, HALF:])
        gate_s[q] = gate
        up_s[q] = up
        hidden = gate * jax.nn.sigmoid(gate) * up
        hw = (weight_col(q) * hidden).astype(BF16)
        hwt[q] = hw.T
        send = pl.multiple_of(other * HALF, HALF)
        keep = pl.multiple_of(core * HALF, HALF)
        by_group(q, lambda k, n: many_x(k, n).wait_send())
        xs[at] = nn(hw, wd[:, pl.ds(send, HALF)]).astype(BF16).reshape(4, T8, 8, HALF)
        many_yp(q, 1).start()
        yo[at] = nn(hw, wd[:, pl.ds(keep, HALF)]).astype(BF16).reshape(4, T8, 8, HALF)

    def cross_y(q):
        many_yp(q, 1).wait_recv()
        at = pl.ds(q * 4, 4)
        send = pl.ds(pl.multiple_of((1 - odd) * QUART, QUART), QUART)
        keep = pl.ds(pl.multiple_of(odd * QUART, QUART), QUART)
        yzo[at] = (yo[at, :, :, send].astype(F32) + ypi[at, :, :, send].astype(F32)).astype(BF16)
        many_yz(q, 1).start()
        yq[at] = (yo[at, :, :, keep].astype(F32) + ypi[at, :, :, keep].astype(F32)).astype(BF16)

    def return_y(q):
        many_yz(q, 1).wait_recv()
        at = pl.ds(q * 4, 4)
        yq[at] = (yq[at].astype(F32) + yzi[at].astype(F32)).astype(BF16)
        loop(jnp.maximum(q * 4, 1), q * 4 + 4, lambda k: many_y(k, 1).start())

    def forward_step(q):
        @pl.when(q < 4)
        def _():
            pass_x(q)

        @pl.when((q >= 1) & (q < 5))
        def _():
            forward(q - 1)

        @pl.when((q >= 2) & (q < 6))
        def _():
            cross_y(q - 2)

        @pl.when(q >= 3)
        def _():
            return_y(q - 3)

    loop(0, 7, forward_step)
    yret[0:1] = yq[0:1]

    def pass_g(q):
        by_group(q, lambda k, n: many_g(k, n).wait_recv())
        cp_gf(q).start()

    def backward(q):
        cp_gf(q).wait_recv()
        at = pl.ds(q * 4, 4)
        dh = nt(rows_of(gr[0, at]), wd[:, :HALF]) + nt(rows_of(gr[1, at]), wd[:, HALF:])
        gate = gate_s[q]
        up = up_s[q]
        sigma = jax.nn.sigmoid(gate)
        silu = gate * sigma
        slope = sigma * (1.0 + gate * (1.0 - sigma))
        dot = jnp.sum(silu * up * dh, axis=1, keepdims=True)
        for r in range(4):
            vs[pl.ds(q * 4 + r, 1)] = to_row(dot[r * CAP : (r + 1) * CAP])[None]
        loop(jnp.maximum(q * 4, 1), q * 4 + 4, lambda k: many_v(k, 1).start())
        dh = weight_col(q) * dh
        dg = (dh * up * slope).astype(BF16)
        du = (dh * silu).astype(BF16)
        dgt[q] = dg.T
        dut[q] = du.T
        dgs[q] = dg
        dus[q] = du

    def backward_step(q):
        @pl.when(q < 4)
        def _():
            pass_g(q)

        @pl.when(q >= 1)
        def _():
            backward(q - 1)

    loop(0, 5, backward_step)

    def input_grad(i):
        p, q = i // 4, i % 4
        at = pl.ds(i * 4, 4)
        send = pl.ds(pl.multiple_of(other * HALF + p * PCOL, PCOL), PCOL)
        keep = pl.ds(pl.multiple_of(core * HALF + p * PCOL, PCOL), PCOL)
        dpo[at] = (nn(dgs[q], wg[:, send]) + nn(dus[q], wu[:, send])).astype(BF16).reshape(4, T8, 8, PCOL)
        many_dp(i, 1).start()
        do[at] = (nn(dgs[q], wg[:, keep]) + nn(dus[q], wu[:, keep])).astype(BF16).reshape(4, T8, 8, PCOL)

    def return_d(i):
        p, q = i // 4, i % 4
        many_dp(i, 1).wait_recv()
        at = pl.ds(i * 4, 4)
        do[at] = (do[at].astype(F32) + dpi[at].astype(F32)).astype(BF16)

        @pl.when(p < 2)
        def _():
            loop(jnp.maximum(q * 4, 1), q * 4 + 4, lambda k: many_d(p, k, 1).start())

    def input_step(i):
        @pl.when(i < 4 * PH)
        def _():
            input_grad(i)

        @pl.when(i >= 1)
        def _():
            return_d(i - 1)

    loop(0, 4 * PH + 1, input_step)
    for p in range(PH):
        dret[p * NDP : p * NDP + 1] = do[p * NDP : p * NDP + 1]
    vret[0:1] = vs[0:1]

    def combine(back, base):
        total = nn(selt[0], rows_of(back[pl.ds(base, 4)]))
        for q in range(1, 4):
            total += nn(selt[q], rows_of(back[pl.ds(base + q * 4, 4)]))
        return total.astype(BF16).reshape(NEX, BLK, back.shape[-1])

    many_y(1, 15).wait_recv()
    mst[...] = combine(yret, 0)
    loop(1, NEX, lambda m: cp_m(m).start())
    mrecv[pl.ds(ex, 1)] = mst[pl.ds(ex, 1)]

    rst[...] = jnp.zeros_like(rst)
    many_v(1, 15).wait_recv()

    def route_grad(k):
        col = to_col(vret[pl.ds(k, 1)][0, 0:1])
        row = jnp.sum(rows_of(sel[pl.ds(k, 1)]).astype(F32) * col, axis=0, keepdims=True)
        add = jnp.where(routes_ref[...] == to_dp(k) * 4 + group, row, 0.0)
        for b in range(4):
            rst[b, :TOP] += add[:, b * 128 : (b + 1) * 128]

    loop(0, NDP, route_grad)
    loop(1, NEX, lambda m: cp_r(m).start())
    rrecv[pl.ds(ex, 1)] = rst[pl.ds(group, 1)]

    def grads(n):
        h = n // (HALF // COLS)
        cols = pl.ds(pl.multiple_of((n % (HALF // COLS)) * COLS, COLS), COLS)
        outs = pl.ds(pl.multiple_of(n * COLS, COLS), COLS)

        def total(left, right):
            acc = nn(left[0], rows_of(right[h, 0:4, :, :, cols]))
            for q in range(1, 4):
                acc += nn(left[q], rows_of(right[h, q * 4 : q * 4 + 4, :, :, cols]))
            return acc.astype(BF16)

        gd[:, outs] = total(hwt, gr)
        gg[:, outs] = total(dgt, xr)
        gu[:, outs] = total(dut, xr)

    def phase(p):
        many_d(p, 1, 15).wait_recv()

        @pl.when(p + 2 < PH)
        def _():
            loop(1, NDP, lambda k: many_d(p + 2, k + core * (NDP - 2 * k), 1).start())

        dst_[pl.ds(p, 1)] = combine(dret, p * NDP)[None]
        loop(1, NEX, lambda m: cp_z(p, m).start())
        drecv[pl.ds(p, 1), pl.ds(ex, 1)] = dst_[pl.ds(p, 1), pl.ds(ex, 1)]
        grads(p)

    loop(0, PH, phase)
    stores = [
        pltpu.make_async_copy(gg, gg_hbm.at[0], out_sem.at[0]),
        pltpu.make_async_copy(gu, gu_hbm.at[0], out_sem.at[1]),
        pltpu.make_async_copy(gd, gd_hbm.at[0], out_sem.at[2]),
    ]
    for store in stores:
        store.start()

    many_m().wait_recv()
    for b in range(4):
        source = (b % 2) * 2 + b // 2
        total = mrecv[source].astype(F32)
        for gg_ in range(1, 4):
            total += mrecv[gg_ * 4 + source].astype(F32)
        mixed_ref[:, b * QUART : (b + 1) * QUART] = total.astype(BF16)
    many_r().wait_recv()
    route_total = jnp.sum(rrecv[...], axis=0)
    mine = jnp.zeros((TOP, BLK), F32)
    for b in range(4):
        mine = jnp.where(ex % 4 == b, route_total[:TOP, b * BLK : (b + 1) * BLK], mine)
    grw_ref[...] = mine
    for p in range(PH):
        many_z(p).wait_recv()
        for h in range(2):
            total = drecv[p, h].astype(F32)
            for zz in range(1, 8):
                total += drecv[p, zz * 2 + h].astype(F32)
            start = h * HALF + p * PCOL
            dx_ref[:, start : start + PCOL] = total.astype(BF16)

    many_gz().wait_send()
    many_w(1, 15).wait_send()
    many_g(1, 15).wait_send()
    cp_all = remote(xr.at[0], xr.at[1], sxf.at[0], rxf.at[0], partner)
    cp_all.wait_send()
    cp_all = remote(gr.at[0], gr.at[1], sgf.at[0], rgf.at[0], partner)
    cp_all.wait_send()
    many_yp(0, 4).wait_send()
    many_yz(0, 4).wait_send()
    many_y(1, 15).wait_send()
    many_dp(0, 4 * PH).wait_send()
    many_v(1, 15).wait_send()
    many_m().wait_send()
    many_r().wait_send()
    for p in range(PH):
        many_d(p, 1, 15).wait_send()
        many_z(p).wait_send()
    for store in stores:
        store.wait()


def hand_over(*refs):
    count = (len(refs) - 2) // 3
    held, (read, write) = refs[2 * count : 3 * count], refs[3 * count :]
    ins = [pltpu.make_async_copy(refs[i], held[i], read.at[i]) for i in range(count)]
    outs = [pltpu.make_async_copy(held[i], refs[count + i], write.at[i]) for i in range(count)]
    for copy in ins:
        copy.start()
    for i in range(count):
        ins[i].wait()
        outs[i].start()
    for copy in outs:
        copy.wait()


def body(tokens, routes, route_weight, w_gate, w_up, w_down, grad_out):
    any_ = pl.BlockSpec(memory_space=pl.ANY)
    vmem = pl.BlockSpec(memory_space=pltpu.VMEM)
    chunk = (NDP, T8, 8, HALF)
    quart = (NDP, T8, 8, QUART)
    phased = (PH * NDP, T8, 8, PCOL)
    dma = pltpu.SemaphoreType.DMA
    V = pltpu.VMEM
    results = pl.pallas_call(
        kernel,
        out_shape=(
            jax.ShapeDtypeStruct((BLK, D), BF16),
            jax.ShapeDtypeStruct((BLK, D), BF16),
            jax.ShapeDtypeStruct((TOP, BLK), F32),
            jax.ShapeDtypeStruct((1, FF, D), BF16),
            jax.ShapeDtypeStruct((1, FF, D), BF16),
            jax.ShapeDtypeStruct((1, FF, D), BF16),
        ),
        in_specs=[any_, vmem, vmem, any_, any_, any_, any_],
        out_specs=(vmem, vmem, vmem, any_, any_, any_),
        scratch_shapes=[
            V((TOK, HALF), BF16), V((2, BLK, HALF), BF16), V((NEX, BLK, HALF), BF16),
            V((FF, D), BF16), V((FF, D), BF16), V((FF, D), BF16),
            V((NDP, TOK), F32), V((NDP, TOK), F32), V((NDP, TOK), F32), V((NDP, T8, 8, TOK), BF16), V((4, TOK, ROWS), BF16),
            V(chunk, BF16), V((2,) + chunk, BF16), V(chunk, BF16), V((2,) + chunk, BF16),
            V((NDP, 8, 128), F32), V((NDP, 8, 128), F32), V((NDP, 8, 128), F32), V((NDP, 8, 128), F32),
            V(chunk, BF16), V(chunk, BF16), V(quart, BF16), V(quart, BF16), V(quart, BF16), V(quart, BF16),
            V(phased, BF16), V(phased, BF16), V(phased, BF16), V(phased, BF16),
            V((4, ROWS, FF), F32), V((4, ROWS, FF), F32),
            V((4, FF, ROWS), BF16), V((4, FF, ROWS), BF16), V((4, FF, ROWS), BF16), V((4, ROWS, FF), BF16), V((4, ROWS, FF), BF16),
            V((NEX, BLK, QUART), BF16), V((NEX, BLK, QUART), BF16), V((PH, NEX, BLK, PCOL), BF16), V((PH, NEX, BLK, PCOL), BF16),
            V((4, 8, 128), F32), V((NEX, 8, 128), F32),
            V((FF, D), BF16), V((FF, D), BF16), V((FF, D), BF16),
            dma((6,)), dma((3,)),
            dma((1,)), dma((1,)), dma((4,)), dma((4,)), dma((1,)), dma((4,)),
            dma((1,)), dma((4,)), dma((1,)), dma((4,)), dma((1,)), dma((4,)),
            dma((1,)), dma((4,)), dma((1,)), dma((4,)), dma((1,)), dma((1,)), dma((1,)), dma((4 * PH,)),
            dma((PH,)), dma((PH,)), dma((1,)), dma((1,)),
            dma((1,)), dma((1,)), dma((PH,)), dma((PH,)), dma((1,)), dma((1,)),
        ],
        compiler_params=pltpu.CompilerParams(
            collective_id=0, has_side_effects=True, vmem_limit_bytes=63_000_000
        ),
    )(tokens, routes.T, route_weight.T, w_gate, w_up, w_down, grad_out)
    mixed, dx, grw, gg, gu, gd = pl.pallas_call(
        hand_over,
        out_shape=tuple(jax.ShapeDtypeStruct(r.shape, r.dtype) for r in results),
        in_specs=[any_] * 6,
        out_specs=(any_,) * 6,
        scratch_shapes=[V(r.shape, r.dtype) for r in results] + [dma((6,)), dma((6,))],
    )(*results)
    return mixed, dx, grw.T, gg, gu, gd


def solution(mesh):
    rows = P(("dp", "expert"), None)
    block = P(("dp", "expert"), None, None)
    return jax.shard_map(
        body,
        mesh=mesh,
        in_specs=(P("dp", None), P("dp", None), P("dp", None), block, block, block, rows),
        out_specs=(rows, rows, rows, block, block, block),
        check_vma=False,
    )
```

time: 189 us -> 147 us (0.78)
  the two profiles are of different devices: /device:TPU:193 before, /device:TPU:1 now
where the time goes in v2:
time: 147 us; the launch traced here: 146 us
  Pallas kernels  146 us (99%)
    pallas_call x1, Pallas kernels, body(): pl.pallas_call(kernel, out_shape=(jax.ShapeDtypeStruct((BLK, D), BF16), j...  142 us
    pallas_call x1, Pallas kernels, body(): pl.pallas_call(hand_over, out_shape=tuple((jax.ShapeDtypeStruct(r.shape,...  3.72 us

profile of v2, /device:TPU:1, one launch (start us, length us, event | category | flops | bytes accessed | tf_op | source)
XLA Modules:
  0.0 146.5 jit_solution(1652523325269166094)
XLA Ops:
  0.6 142.1 %shard_map.118 = (bf16[32,2048]{1,0:T(8,128)(2,1)}, bf16[32,2048]{1,0:T(8,128)(2,1)}, f32[6,32]{1,0:T(8,128)}, bf16[1,352,2048]{2,1,0:T(8,128)(2,1)}, bf16[1,352...) custom-call(bf16[512,2048]{1,0:T(8,128)(2,1)} %tok_hbm.1, s32[6,512]{1,0:T(8,128)} %bitcast.3, f32[6,512]{1,0:T(8,128)} %bitcast.4, ...), custom_call_target="tpu_custom_call" | custom-call | tf_op jit(solution)/shard_map/pallas_call | solution.py:515
  142.8 3.7 %shard_map.119 = (bf16[32,2048]{1,0:T(8,128)(2,1)}, bf16[32,2048]{1,0:T(8,128)(2,1)}, f32[6,32]{1,0:T(8,128)}, bf16[1,352,2048]{2,1,0:T(8,128)(2,1)}, bf16[1,352...) custom-call(bf16[32,2048]{1,0:T(8,128)(2,1)} %get-tuple-element.18.refs_0_, ...), custom_call_target="tpu_custom_call" | custom-call | tf_op jit(solution)/shard_map/pallas_call | solution.py:551

commit v3 on v2

--- a/solution.py
+++ b/solution.py
@@ -49,9 +49,9 @@
     xs, xr, gs, gr, ws, wr, vs, vret,
     yo, ypi, yzo, yzi, yq, yret, do, dpo, dpi, dret,
     gate_s, up_s, hwt, dgt, dut, dgs, dus,
-    mst, mrecv, dst_, drecv, rst, rrecv, gg, gu, gd,
+    mst, mrecv, dst_, pre, drecv, rst, rrecv, gg, gu, gd,
     in_sem, out_sem, sgz, rgz, sx, rx, sxf, rxf, sw, rw, sg, rg, sgf, rgf,
-    syp, ryp, syz, ryz, sy, ry, sdp, rdp, sd, rd, sv, rv, sm, rm, sz, rz, sr, rr,
+    syp, ryp, syz, ryz, sy, ry, sdp, rdp, sd, rd, sv, rv, sm, rm, spre, rpre, sz, rz, sr, rr,
 ):
     dp = lax.axis_index("dp")
     ex = lax.axis_index("expert")
@@ -60,7 +60,8 @@
     other = 1 - core
     group = ex // 4
     partner = (dp, ex + 1 - 2 * core)
-    odd = (ex // 2) % 2
+    ez = ex // 2
+    odd = ez % 2
     across = (dp, ex + 2 - 4 * odd)
 
     def gray(v):
@@ -139,13 +140,23 @@
     def many_m():
         return remote(mst.at[pl.ds(0, 15)], mrecv.at[pl.ds(0, 15)], sm.at[0], rm.at[0], partner)
 
-    def cp_z(p, m):
-        e2 = to_ex(m)
-        return remote(dst_.at[p, e2], drecv.at[p, ex], sz.at[p], rz.at[p], (dp, e2))
+    def chip(n, z, c):
+        return (z + (1 - 2 * c) * n + 8) % 8
+
+    def cp_pre(p, i, d, to):
+        src = dst_.at[p, pl.ds(2 * chip(d, ez, core), 2)]
+        return remote(src, pre.at[p, i], spre.at[p], rpre.at[p], (dp, 2 * chip(to, ez, core) + core))
+
+    def many_pre(p):
+        return remote(pre.at[p], pre.at[p], spre.at[p], rpre.at[p], partner)
+
+    def cp_z(p, i, d, c2):
+        e2 = 2 * chip(d, ez, core) + c2
+        return remote(dst_.at[p, e2], drecv.at[p, core * 5 + i], sz.at[p], rz.at[p], (dp, e2))
 
     def many_z(p):
-        at = pl.ds(0, 15)
-        return remote(dst_.at[p, at], drecv.at[p, at], sz.at[p], rz.at[p], partner)
+        at = pl.ds(0, 9)
+        return remote(drecv.at[p, at], drecv.at[p, at], sz.at[p], rz.at[p], partner)
 
     def cp_r(m):
         e2 = to_ex(m)
@@ -368,7 +379,7 @@
         at = pl.ds(i * 4, 4)
         do[at] = (do[at].astype(F32) + dpi[at].astype(F32)).astype(BF16)
 
-        @pl.when(p < 2)
+        @pl.when(p < 1)
         def _():
             loop(jnp.maximum(q * 4, 1), q * 4 + 4, lambda k: many_d(p, k, 1).start())
 
@@ -392,7 +403,11 @@
             total += nn(selt[q], rows_of(back[pl.ds(base + q * 4, 4)]))
         return total.astype(BF16).reshape(NEX, BLK, back.shape[-1])
 
+    def go_d(p):
+        loop(1, NDP, lambda k: many_d(p, k + core * (NDP - 2 * k), 1).start())
+
     many_y(1, 15).wait_recv()
+    go_d(1)
     mst[...] = combine(yret, 0)
     loop(1, NEX, lambda m: cp_m(m).start())
     mrecv[pl.ds(ex, 1)] = mst[pl.ds(ex, 1)]
@@ -426,19 +441,42 @@
         gg[:, outs] = total(dgt, xr)
         gu[:, outs] = total(dut, xr)
 
+    def arrive(p):
+        many_d(p, 1, 15).wait_recv()
+
+        @pl.when(p + 2 < PH)
+        def _():
+            go_d(p + 2)
+
+        dst_[pl.ds(p, 1)] = combine(dret, p * NDP)[None]
+        cp_pre(p, 0, -4, -1).start()
+        cp_pre(p, 1, -2, -1).start()
+        cp_pre(p, 2, 3, 1).start()
+        cp_z(p, 3, 1, 0).start()
+        cp_z(p, 3, 1, 1).start()
+        cp_z(p, 4, 0, other).start()
+        drecv[pl.ds(p, 1), pl.ds(core * 5 + 4, 1)] = dst_[pl.ds(p, 1), pl.ds(ex, 1)]
+        grads(p)
+
+    def pass_on(p):
+        many_pre(p).wait_recv()
+        for i, d in ((0, -3), (1, -1), (2, 2)):
+            at = pl.ds(2 * chip(d, ez, core), 2)
+            joined = dst_[pl.ds(p, 1), at].astype(F32) + pre[pl.ds(p, 1), i].astype(F32)
+            dst_[pl.ds(p, 1), at] = joined.astype(BF16)
+            cp_z(p, i, d, 0).start()
+            cp_z(p, i, d, 1).start()
+
     def phase(p):
-        many_d(p, 1, 15).wait_recv()
-
-        @pl.when(p + 2 < PH)
-        def _():
-            loop(1, NDP, lambda k: many_d(p + 2, k + core * (NDP - 2 * k), 1).start())
-
-        dst_[pl.ds(p, 1)] = combine(dret, p * NDP)[None]
-        loop(1, NEX, lambda m: cp_z(p, m).start())
-        drecv[pl.ds(p, 1), pl.ds(ex, 1)] = dst_[pl.ds(p, 1), pl.ds(ex, 1)]
-        grads(p)
-
-    loop(0, PH, phase)
+        @pl.when(p < PH)
+        def _():
+            arrive(p)
+
+        @pl.when(p >= 1)
+        def _():
+            pass_on(p - 1)
+
+    loop(0, PH + 1, phase)
     stores = [
         pltpu.make_async_copy(gg, gg_hbm.at[0], out_sem.at[0]),
         pltpu.make_async_copy(gu, gu_hbm.at[0], out_sem.at[1]),
@@ -463,9 +501,9 @@
     for p in range(PH):
         many_z(p).wait_recv()
         for h in range(2):
-            total = drecv[p, h].astype(F32)
-            for zz in range(1, 8):
-                total += drecv[p, zz * 2 + h].astype(F32)
+            total = drecv[p, 5 * h].astype(F32)
+            for i in range(1, 5):
+                total += drecv[p, 5 * h + i].astype(F32)
             start = h * HALF + p * PCOL
             dx_ref[:, start : start + PCOL] = total.astype(BF16)
 
@@ -485,6 +523,7 @@
     many_r().wait_send()
     for p in range(PH):
         many_d(p, 1, 15).wait_send()
+        many_pre(p).wait_send()
         many_z(p).wait_send()
     for store in stores:
         store.wait()
@@ -534,7 +573,7 @@
             V(phased, BF16), V(phased, BF16), V(phased, BF16), V(phased, BF16),
             V((4, ROWS, FF), F32), V((4, ROWS, FF), F32),
             V((4, FF, ROWS), BF16), V((4, FF, ROWS), BF16), V((4, FF, ROWS), BF16), V((4, ROWS, FF), BF16), V((4, ROWS, FF), BF16),
-            V((NEX, BLK, QUART), BF16), V((NEX, BLK, QUART), BF16), V((PH, NEX, BLK, PCOL), BF16), V((PH, NEX, BLK, PCOL), BF16),
+            V((NEX, BLK, QUART), BF16), V((NEX, BLK, QUART), BF16), V((PH, NEX, BLK, PCOL), BF16), V((PH, 3, 2, BLK, PCOL), BF16), V((PH, 10, BLK, PCOL), BF16),
             V((4, 8, 128), F32), V((NEX, 8, 128), F32),
             V((FF, D), BF16), V((FF, D), BF16), V((FF, D), BF16),
             dma((6,)), dma((3,)),
@@ -542,7 +581,7 @@
             dma((1,)), dma((4,)), dma((1,)), dma((4,)), dma((1,)), dma((4,)),
             dma((1,)), dma((4,)), dma((1,)), dma((4,)), dma((1,)), dma((1,)), dma((1,)), dma((4 * PH,)),
             dma((PH,)), dma((PH,)), dma((1,)), dma((1,)),
-            dma((1,)), dma((1,)), dma((PH,)), dma((PH,)), dma((1,)), dma((1,)),
+            dma((1,)), dma((1,)), dma((PH,)), dma((PH,)), dma((PH,)), dma((PH,)), dma((1,)), dma((1,)),
         ],
         compiler_params=pltpu.CompilerParams(
             collective_id=0, has_side_effects=True, vmem_limit_bytes=63_000_000

time: 147 us -> 144 us (0.980)
  Pallas kernels: 146 us -> 143 us
    pallas_call x1, Pallas kernels: 142 us -> 140 us  [body(): pl.pallas_call(kernel, out_shape=(jax.ShapeDtypeStruct((BLK, D), BF16), j...]
where the time goes in v3:
time: 144 us
  Pallas kernels  143 us (99%)
    pallas_call x1, Pallas kernels, body(): pl.pallas_call(kernel, out_shape=(jax.ShapeDtypeStruct((BLK, D), BF16), j...  140 us
    pallas_call x1, Pallas kernels, body(): pl.pallas_call(hand_over, out_shape=tuple((jax.ShapeDtypeStruct(r.shape,...  3.72 us

profile of v3, /device:TPU:1, one launch (start us, length us, event | category | flops | bytes accessed | tf_op | source)
XLA Modules:
  0.0 144.0 jit_solution(7124835538129727202)
XLA Ops:
  0.6 139.7 %shard_map.118 = (bf16[32,2048]{1,0:T(8,128)(2,1)}, bf16[32,2048]{1,0:T(8,128)(2,1)}, f32[6,32]{1,0:T(8,128)}, bf16[1,352,2048]{2,1,0:T(8,128)(2,1)}, bf16[1,352...) custom-call(bf16[512,2048]{1,0:T(8,128)(2,1)} %tok_hbm.1, s32[6,512]{1,0:T(8,128)} %bitcast.3, f32[6,512]{1,0:T(8,128)} %bitcast.4, ...), custom_call_target="tpu_custom_call" | custom-call | tf_op jit(solution)/shard_map/pallas_call | solution.py:554
  140.3 3.7 %shard_map.119 = (bf16[32,2048]{1,0:T(8,128)(2,1)}, bf16[32,2048]{1,0:T(8,128)(2,1)}, f32[6,32]{1,0:T(8,128)}, bf16[1,352,2048]{2,1,0:T(8,128)(2,1)}, bf16[1,352...) custom-call(bf16[32,2048]{1,0:T(8,128)(2,1)} %get-tuple-element.18.refs_0_, ...), custom_call_target="tpu_custom_call" | custom-call | tf_op jit(solution)/shard_map/pallas_call | solution.py:590

commit v4 on v3

--- a/solution.py
+++ b/solution.py
@@ -250,7 +250,7 @@
         loop(jnp.maximum(q * 4, 1), q * 4 + 4, go)
         selt[q] = s.T
 
-    loop(0, 4, send_x)
+    loop(0, 4, lambda q: send_x(q + core * (3 - 2 * q)))
     xr[pl.ds(core, 1), 0:1] = xs[0:1][None]
     wr[0:1] = ws[0:1]
 
@@ -259,14 +259,15 @@
     def send_g(q):
         at = pl.ds(q * 4, 4)
         gs[at] = nn(rows_of(sel[at]), rows_of(gall[...])).astype(BF16).reshape(4, T8, 8, HALF)
-        loop(jnp.maximum(q * 4, 1), q * 4 + 4, lambda k: many_g(k, 1).start())
+        lo, hi = jnp.maximum(q * 4, 1), q * 4 + 4
+        loop(lo, hi, lambda k: many_g(k + core * (lo + hi - 1 - 2 * k), 1).start())
 
     def pass_x(q):
         by_group(q, lambda k, n: many_x(k, n).wait_recv())
         by_group(q, lambda k, n: many_w(k, n).wait_recv())
         cp_xf(q).start()
 
-    loop(0, 4, send_g)
+    loop(0, 4, lambda q: send_g(q + core * (3 - 2 * q)))
     gr[pl.ds(core, 1), 0:1] = gs[0:1][None]
     for load in loads[3:]:
         load.wait()

time: 144 us -> 137 us (0.951)
  Pallas kernels: 143 us -> 136 us
    pallas_call x1, Pallas kernels: 140 us -> 133 us  [body(): pl.pallas_call(kernel, out_shape=(jax.ShapeDtypeStruct((BLK, D), BF16), j...]
where the time goes in v4:
time: 137 us
  Pallas kernels  136 us (99%)
    pallas_call x1, Pallas kernels, body(): pl.pallas_call(kernel, out_shape=(jax.ShapeDtypeStruct((BLK, D), BF16), j...  133 us
    pallas_call x1, Pallas kernels, body(): pl.pallas_call(hand_over, out_shape=tuple((jax.ShapeDtypeStruct(r.shape,...  3.72 us

profile of v4, /device:TPU:1, one launch (start us, length us, event | category | flops | bytes accessed | tf_op | source)
XLA Modules:
  0.0 137.0 jit_solution(10570193928179620742)
XLA Ops:
  0.6 132.6 %shard_map.118 = (bf16[32,2048]{1,0:T(8,128)(2,1)}, bf16[32,2048]{1,0:T(8,128)(2,1)}, f32[6,32]{1,0:T(8,128)}, bf16[1,352,2048]{2,1,0:T(8,128)(2,1)}, bf16[1,352...) custom-call(bf16[512,2048]{1,0:T(8,128)(2,1)} %tok_hbm.1, s32[6,512]{1,0:T(8,128)} %bitcast.3, f32[6,512]{1,0:T(8,128)} %bitcast.4, ...), custom_call_target="tpu_custom_call" | custom-call | tf_op jit(solution)/shard_map/pallas_call | solution.py:555
  133.2 3.7 %shard_map.119 = (bf16[32,2048]{1,0:T(8,128)(2,1)}, bf16[32,2048]{1,0:T(8,128)(2,1)}, f32[6,32]{1,0:T(8,128)}, bf16[1,352,2048]{2,1,0:T(8,128)(2,1)}, bf16[1,352...) custom-call(bf16[32,2048]{1,0:T(8,128)(2,1)} %get-tuple-element.18.refs_0_, ...), custom_call_target="tpu_custom_call" | custom-call | tf_op jit(solution)/shard_map/pallas_call | solution.py:591
